TPU v7x, 32 devices: a whole 2x2x4 slice. The times are simulated.
32 devices in a mesh: groups: 2 (over x), dp: 8 (over z, y), tensor: 2 (over core).
Axes of the slice: x: 2, y: 2, z: 4, core: 2. Of those that a mesh axis runs over, the one named last changes fastest.
Arguments:
- hidden: bfloat16 [2048, 8192], P(('groups', 'dp'), 'tensor'), parts along dimension 0, may hold values from -6 to 6
- row_adapter_index: int32 [2048, 1], P(('groups', 'dp')), parts along dimension 0, may hold values from 0 to 15; in each aligned block of 128 rows (0 to 127, 128 to 255, ...) at most 16 rows name the same one
- key_value_weight: bfloat16 [8192, 2048], P('tensor'), may hold values from -0.0625 to 0.0625
- adapter_down_weight: bfloat16 [32, 8192, 128], P(('groups', 'dp'), 'tensor'), parts along dimension 0, may hold values from -0.0625 to 0.0625
- adapter_up_weight: bfloat16 [32, 2, 64, 1024], P(('groups', 'dp')), parts along dimension 0, may hold values from -0.75 to 0.75
Outputs:
- new_kv: bfloat16 [2048, 2048], P(('groups', 'dp'), 'tensor'), parts along dimension 0
There are 2 independent parts, one for each index of `groups`. A program takes and returns all parts, laid end to end along the dimension named above; an argument that names none is the same for every part. Nothing has to cross between parts.
Inputs may be any that keep to these rules, and one draw needn't show every extreme that they name: `row_adapter_index`: within the 128 rows of one dp index (aligned blocks of rows), no adapter is named by more than 16 rows, a bound that some block reaches.
All inputs are finite; a program needn't handle non-finite values.
Results may differ from a plain program's by a relative error of at most 0.001.
Values may be sent and summed in bfloat16 or wider, within the bound.
A program may use at most 64 MiB of HBM per device.

v0:
```python
import jax
import jax.numpy as jnp
from jax import lax
from jax.sharding import PartitionSpec as P

CAP = 16


def per_device(hidden, row_adapter_index, key_value_weight, adapter_down_weight, adapter_up_weight):
    dp_count = lax.axis_size("dp")
    replica_adapters = adapter_down_weight.shape[0]
    adapters_all = replica_adapters * dp_count
    slot_count = adapters_all * CAP
    chosen_adapter = row_adapter_index[:, 0]
    one_hot = (
        chosen_adapter[:, None] == jnp.arange(adapters_all, dtype=jnp.int32)[None, :]
    ).astype(jnp.int32)
    earlier = jnp.cumsum(one_hot, axis=0) - one_hot
    position = jnp.sum(earlier * one_hot, axis=1)
    slot_index = chosen_adapter * CAP + position
    placement_map = (
        jnp.arange(slot_count, dtype=jnp.int32)[:, None] == slot_index[None, :]
    ).astype(jnp.bfloat16)
    packed = jnp.dot(placement_map, hidden, preferred_element_type=jnp.float32).astype(jnp.bfloat16)
    packed = packed.reshape(dp_count, replica_adapters, CAP, hidden.shape[1])
    rank_length = adapter_up_weight.shape[2]
    key_value_width = adapter_up_weight.shape[3]
    tensor_count = lax.axis_size("tensor")
    lane_width = 2 * key_value_width // tensor_count
    lane_index = lax.axis_index("tensor")
    lane_start = lane_index * lane_width
    projection_output = lane_start // key_value_width
    shrink = jnp.einsum(
        "sjcd,jdr->sjcr",
        lax.all_to_all(packed, "dp", split_axis=0, concat_axis=0, tiled=True),
        adapter_down_weight,
        preferred_element_type=jnp.float32,
    )
    shrink = lax.psum(shrink, "tensor")
    shrink_lane = lax.dynamic_slice_in_dim(shrink, projection_output * rank_length, rank_length, 3)
    selected_up_weight = lax.dynamic_index_in_dim(
        adapter_up_weight, projection_output, 1, keepdims=False
    )
    up_lane = selected_up_weight.astype(jnp.float32)
    delta_lane = jnp.einsum("sjcr,jrk->sjck", shrink_lane, up_lane, precision=lax.Precision.HIGHEST)
    returned = lax.all_to_all(delta_lane, "dp", split_axis=0, concat_axis=0, tiled=True)
    returned = returned.reshape(slot_count, returned.shape[-1])
    per_row = jnp.take(returned, slot_index, axis=0)
    base_partial = jnp.dot(hidden, key_value_weight, preferred_element_type=jnp.float32)
    summed = lax.psum_scatter(base_partial, "tensor", scatter_dimension=1, tiled=True)
    summed = summed + per_row
    return summed.astype(jnp.bfloat16)


def solution(mesh):
    in_specs = (
        P(("groups", "dp"), "tensor"),
        P(("groups", "dp"), None),
        P("tensor", None),
        P(("groups", "dp"), "tensor", None),
        P(("groups", "dp"), None, None, None),
    )
    out_specs = P(("groups", "dp"), "tensor")
    return jax.shard_map(
        per_device, mesh=mesh, in_specs=in_specs, out_specs=out_specs, check_vma=False
    )
```

profile of v0, /device:TPU:0, one launch (start us, length us, event | category | flops | bytes accessed | tf_op | source)
XLA Modules:
  0.0 130.1 jit_solution(16295724948775301776)
XLA Ops:
  6.5 0.0 copy-start
  6.5 0.0 all-reduce.2.cloned.1.call-start
  6.5 0.9 fusion.12
  7.4 0.2 reduce_window_sum.11
  7.6 0.8 select_reduce_fusion
  8.4 0.7 multiply_add_fusion
  9.1 1.9 %convolution_convert_fusion = bf16[256,4096]{1,0:T(8,128)(2,1)S(1)} fusion(bf16[128,4096]{1,0:T(8,128)(2,1)} %param.5, s32[128]{0:T(128)S(1)} %multiply_add_fusion), kind=kOutput, calls=%fused_computation.1 | convolution fusion | flops 269516800 | bytes 3146240 | tf_op jit(solution)/shard_map/dot_general | solution.py:24
  11.0 55.3 %all_to_all.10 = bf16[8,2,16,4096]{3,2,1,0:T(8,128)(2,1)S(1)} all-to-all(bf16[8,2,16,4096]{3,2,1,0:T(8,128)(2,1)S(1)} %bitcast.33), channel_id=1, replica_groups=mesh['groups'=2,'dp'=8,'tensor'=2] {'dp'}, dimensions={0} | all-to-all | bytes 4194304 | tf_op jit(solution)/shard_map/all_to_all | solution.py:35
  66.3 0.0 copy-done
  66.3 0.0 copy-start.1
  66.4 1.4 %fusion.3 = f32[8,2,16,128]{3,2,0,1:T(8,128)} fusion(bf16[2,4096,128]{2,1,0:T(8,128)(2,1)S(1)} %copy-done, bf16[8,2,16,4096]{3,2,1,0:T(8,128)(2,1)S(1)} %all_to_all.10), kind=kOutput, calls=%fused_computation.6 | convolution fusion | flops 268435456 | bytes 4325376 | tf_op jit(solution)/shard_map/sjcd,jdr->sjcr/dot_general | solution.py:33
  67.7 0.0 all-reduce.2.cloned.1.call-update
  67.8 0.0 reduce-scatter.2.cloned.1.call-start
  67.8 0.0 copy-done.1
  67.8 9.1 %fusion.14 = f32[128,2048]{1,0:T(8,128)} fusion(bf16[128,4096]{1,0:T(8,128)(2,1)S(1)} %copy-done.1, bf16[4096,2048]{1,0:T(8,128)(2,1)} %param.7), kind=kOutput, calls=%fused_computation.22 | convolution fusion | flops 2147483648 | bytes 18874368 | tf_op jit(solution)/shard_map/dot_general | solution.py:49
  77.0 0.0 reduce-scatter.2.cloned.1.call-update
  77.0 7.8 %all-reduce.2.cloned.1.call-done = f32[8,2,16,128]{3,2,0,1:T(8,128)} async-done(((f32[8,2,16,128]{3,2,0,1:T(8,128)}), f32[8,2,16,128]{3,2,0,1:T(8,128)}) %all-reduce.2.cloned.1.call-update) | async-done | bytes 131088 | tf_op jit(solution)/shard_map/psum | solution.py:39
  84.9 1.6 %convolution_bitcast_fusion = f32[8,2,16,1024]{3,2,0,1:T(8,128)S(1)} fusion(bf16[2,2,64,1024]{3,2,1,0:T(8,128)(2,1)} %param.9, s32[]{:T(128)S(6)} %select_n.25, f32[8,2,16,128]{3,2,0,1:T(8,128)} %all-reduce.2.cloned.1.call-done, s32[]{:T(128)S(6)} %select_n.26), kind=kOutput, calls=%fused_computation.5 | convolution fusion | flops 201326592 | bytes 1441800 | tf_op jit(solution)/shard_map/sjcr,jrk->sjck/dot_general | solution.py:45
  86.5 0.0 copy-start.2
  86.5 1.1 copy.10
  87.6 5.8 %all-to-all-start.1 = ((f32[8,2,16,1024]{3,2,1,0:T(8,128)}), f32[8,2,16,1024]{3,2,1,0:T(8,128)S(1)}, u32[]{:S(2)}, u32[]{:S(2)}) async-start(f32[8,2,16,1024]{3,2,1,0:T(8,128)} %copy.10), calls=%async_computation.2 | async-start | bytes 2097152 | tf_op jit(solution)/shard_map/all_to_all | solution.py:46
  93.4 0.0 copy-done.2
  93.5 26.2 %all-to-all-done.1 = f32[8,2,16,1024]{3,2,1,0:T(8,128)S(1)} async-done(((f32[8,2,16,1024]{3,2,1,0:T(8,128)}), f32[8,2,16,1024]{3,2,1,0:T(8,128)S(1)}, u32[]{:S(2)}, u32[]{:S(2)}) %all-to-all-start.1) | async-done | bytes 1048608 | tf_op jit(solution)/shard_map/all_to_all | solution.py:46
  119.7 1.6 %gather_fusion = f32[128,1024]{1,0:T(8,128)} fusion(f32[256,1024]{1,0:T(8,128)S(1)} %bitcast.32, s32[1024]{0:T(1024)S(1)} %pad_clamp_fusion), kind=kCustom, calls=%fused_computation | custom fusion | bytes 1049088 | tf_op jit(solution)/shard_map/jit(_take)/gather | solution.py:48
  121.3 0.0 reduce-scatter.2.cloned.1.call-done
  121.3 2.0 %add_convert_fusion = bf16[128,1024]{1,0:T(8,128)(2,1)} fusion(f32[128,1024]{1,0:T(8,128)} %reduce-scatter.2.cloned.1.call-done, f32[128,1024]{1,0:T(8,128)} %gather_fusion, pred[128]{0:T(512)(128)(4,1)S(1)} %get-tuple-element.5), kind=kLoop, calls=%fused_computation.7 | loop fusion | flops 393216 | bytes 1310848 | tf_op jit(solution)/shard_map/convert_element_type | solution.py:52
  (2 shorter events, 0.0 us)
Async XLA Ops:
  6.5 59.8 %copy-start = (bf16[2,4096,128]{2,1,0:T(8,128)(2,1)S(1)}, bf16[2,4096,128]{2,1,0:T(8,128)(2,1)}, u32[]{:S(2)}) copy-start(bf16[2,4096,128]{2,1,0:T(8,128)(2,1)} %param.8) | copy-start | bytes 6291460
  6.5 78.3 %all-reduce.2.cloned.1.call-start = ((), (), s32[]{:S(2)}) async-start(), calls=%async_computation.4 | async-start | bytes 262144 | tf_op jit(solution)/shard_map/psum | solution.py:39
  66.3 1.5 %copy-start.1 = (bf16[128,4096]{1,0:T(8,128)(2,1)S(1)}, bf16[128,4096]{1,0:T(8,128)(2,1)}, u32[]{:S(2)}) copy-start(bf16[128,4096]{1,0:T(8,128)(2,1)} %param.5) | copy-start | bytes 3145732
  67.8 53.5 %reduce-scatter.2.cloned.1.call-start = ((), (), s32[]{:S(2)}) async-start(), calls=%async_computation.3 | async-start | bytes 1572864 | tf_op jit(solution)/shard_map/reduce_scatter | solution.py:50
  86.5 6.9 %copy-start.2 = (s32[128,1]{0,1:T(1,128)S(1)}, s32[128,1]{0,1:T(1,128)}, u32[]{:S(2)}) copy-start(s32[128,1]{0,1:T(1,128)} %param.6) | copy-start | bytes 1540
  87.6 32.0 %all-to-all-start.1 = ((f32[8,2,16,1024]{3,2,1,0:T(8,128)}), f32[8,2,16,1024]{3,2,1,0:T(8,128)S(1)}, u32[]{:S(2)}, u32[]{:S(2)}) async-start(f32[8,2,16,1024]{3,2,1,0:T(8,128)} %copy.10), calls=%async_computation.2 | async-start | bytes 2097152 | tf_op jit(solution)/shard_map/all_to_all | solution.py:46
Sparse Core Ops, SparseCore 0:
  67.9 16.9 all-reduce.1
  87.1 9.6 reduce-scatter.1
where the time goes:
time: 130 us
  blocking collectives  55.3 us (43%)
  waiting for transfers between devices  34.1 us (26%)
  matrix products  14.1 us (11%)
  between operations  13.5 us (10%)
  starting transfers between devices  5.81 us (4%)
  other arithmetic  4.58 us (4%)
  local copies, waits for them, and re-layouts  2.76 us (2%)
    all_to_all x1, blocking collectives, per_device(): lax.all_to_all(packed, 'dp', split_axis=0, concat_axis=0, tiled=True)  55.3 us
    all_to_all x1, waiting for transfers between devices, per_device(): lax.all_to_all(delta_lane, 'dp', split_axis=0, concat_axis=0, tiled=True)  26.2 us
    dot_general x1, matrix products, per_device(): jnp.dot(hidden, key_value_weight, preferred_element_type=jnp.float32)  9.14 us
    psum x1, waiting for transfers between devices, per_device(): shrink = lax.psum(shrink, 'tensor')  7.85 us
    all_to_all x1, starting transfers between devices, per_device(): lax.all_to_all(delta_lane, 'dp', split_axis=0, concat_axis=0, tiled=True)  5.77 us
  transfers between devices with their start and end apart: 3, of which 2 were waited for; matrix products, arithmetic and copies ran while one was open for 10% of the time, Pallas kernels for 0%

commit v1 on v0

v1 whole, which is shorter than its diff:
```python
import functools

import jax
import jax.numpy as jnp
from jax import lax
from jax.experimental import pallas as pl
from jax.experimental.pallas import tpu as pltpu
from jax.sharding import PartitionSpec as P

CAP = 16
MESH = pl.DeviceIdType.MESH
FEATURE_CHUNKS = 4
WEIGHT_CHUNKS = 8


def partner(me, offset):
    other, bit = me, 1
    while bit <= offset:
        if offset & bit:
            other = other + bit - 2 * bit * ((me // bit) % 2)
        bit *= 2
    return other


def kernel(
    n, index_ref, hidden_hbm, weight_hbm, down_hbm, up_hbm, out_ref,
    hidden, weight, down, up, packed, arrived, total, base_arrived, shrink, shrink_out, shrink_in,
    load_hidden, load_weight, load_down, load_up,
    row_send, row_recv, up_send, up_recv, back_send, back_recv, base_send, base_recv,
):
    me = lax.axis_index("dp")
    core = lax.axis_index("tensor")
    sibling = 1 - core
    rows, width = hidden.shape
    adapters = down.shape[0]
    rank = up_hbm.shape[2]
    lanes = up.shape[2]
    chunk = width // FEATURE_CHUNKS
    depth = width // WEIGHT_CHUNKS
    slots = adapters * CAP

    def hidden_load(c):
        part = pl.ds(c * chunk, chunk)
        return pltpu.make_async_copy(hidden_hbm.at[:, part], hidden.at[:, part], load_hidden.at[c])

    def weight_load(k):
        part = pl.ds(k * depth, depth)
        return pltpu.make_async_copy(weight_hbm.at[part], weight.at[part], load_weight.at[k])

    def up_load(j):
        return pltpu.make_async_copy(
            up_hbm.at[j, core], up.at[me, pl.ds(j * rank, rank)], load_up.at[j]
        )

    down_load = pltpu.make_async_copy(down_hbm, down, load_down)
    for c in range(FEATURE_CHUNKS):
        hidden_load(c).start()
    for j in range(adapters):
        up_load(j).start()
    for k in range(WEIGHT_CHUNKS):
        weight_load(k).start()
    down_load.start()

    barrier = pltpu.get_barrier_semaphore()
    for offset in range(n):
        for other in range(2):
            if offset or other:
                pl.semaphore_signal(
                    barrier, inc=1, device_id_type=MESH,
                    device_id={"dp": partner(me, offset), "tensor": sibling if other else core},
                )

    chosen = index_ref[...]
    one_hot = chosen == lax.broadcasted_iota(jnp.int32, (rows, adapters * n), 1)
    one_hot = jnp.where(one_hot, 1.0, 0.0)
    below = lax.broadcasted_iota(jnp.int32, (rows, rows), 0) > lax.broadcasted_iota(
        jnp.int32, (rows, rows), 1
    )
    earlier = jnp.dot(
        jnp.where(below, 1.0, 0.0).astype(jnp.bfloat16), one_hot.astype(jnp.bfloat16),
        preferred_element_type=jnp.float32,
    )
    position = jnp.sum(earlier * one_hot, axis=1, keepdims=True).astype(jnp.int32)
    slot = chosen * CAP + position
    placement = jnp.where(
        slot == lax.broadcasted_iota(jnp.int32, (rows, n * slots), 1), 1.0, 0.0
    ).T.astype(jnp.bfloat16)

    for j in range(adapters):
        up_load(j).wait()
    pl.semaphore_wait(barrier, 2 * n - 1)

    def up_copy(offset, step):
        block = partner(me, offset ^ step)
        return pltpu.make_async_remote_copy(
            src_ref=up.at[block], dst_ref=up.at[block],
            send_sem=up_send.at[offset], recv_sem=up_recv.at[offset],
            device_id={"dp": partner(me, step)}, device_id_type=MESH,
        )

    def up_arrival(offset):
        block = up.at[partner(me, offset)]
        return pltpu.make_async_remote_copy(
            src_ref=block, dst_ref=block,
            send_sem=up_send.at[offset], recv_sem=up_recv.at[offset],
            device_id={"dp": partner(me, 1)}, device_id_type=MESH,
        )

    steps = []
    step = n // 2
    while step:
        steps.append((step, [step + held for held in range(0, n, 2 * step)]))
        step //= 2

    def up_start(number):
        step, offsets = steps[number]
        for offset in offsets:
            up_copy(offset, step).start()

    def up_wait(number):
        for offset in steps[number][1]:
            up_arrival(offset).wait_recv()

    order = sorted(range(1, n), reverse=True)

    def row_copy(c, offset):
        target = partner(me, offset)
        return pltpu.make_async_remote_copy(
            src_ref=packed.at[c, target], dst_ref=arrived.at[c, me],
            send_sem=row_send.at[c, offset], recv_sem=row_recv.at[c, offset],
            device_id={"dp": target}, device_id_type=MESH,
        )

    def row_arrival(c, offset):
        return pltpu.make_async_remote_copy(
            src_ref=packed.at[c, 0], dst_ref=arrived.at[c, partner(me, offset)],
            send_sem=row_send.at[c, offset], recv_sem=row_recv.at[c, offset],
            device_id={"dp": partner(me, offset)}, device_id_type=MESH,
        )

    def rows_start(c):
        hidden_load(c).wait()
        block = jnp.dot(
            placement, hidden[:, c * chunk:(c + 1) * chunk], preferred_element_type=jnp.float32
        ).astype(jnp.bfloat16)
        packed[c] = block.reshape(n, slots, chunk)
        for offset in order:
            row_copy(c, offset).start()
        arrived[c, me] = packed[c, me]

    def rows_use(c):
        for offset in order:
            row_arrival(c, offset).wait_recv()
        for j in range(adapters):
            taken = arrived[c, :, j * CAP:(j + 1) * CAP, :].reshape(n * CAP, chunk)
            part = jnp.dot(
                taken, down[j, c * chunk:(c + 1) * chunk, :], preferred_element_type=jnp.float32
            )
            if c == 0:
                shrink[j] = part
            else:
                shrink[j] += part

    up_start(0)
    for c in range(FEATURE_CHUNKS):
        rows_start(c)

    for k in range(WEIGHT_CHUNKS):
        weight_load(k).wait()
        for half in range(2):
            part = jnp.dot(
                hidden[:, k * depth:(k + 1) * depth],
                weight[k * depth:(k + 1) * depth, half * lanes:(half + 1) * lanes],
                preferred_element_type=jnp.float32,
            )
            if k == 0:
                total[half] = part
            else:
                total[half] += part
    base_copy = pltpu.make_async_remote_copy(
        src_ref=total.at[sibling], dst_ref=base_arrived, send_sem=base_send, recv_sem=base_recv,
        device_id={"tensor": sibling}, device_id_type=MESH,
    )
    base_copy.start()

    down_load.wait()
    for number in range(len(steps) - 1):
        up_wait(number)
        up_start(number + 1)
    for c in range(FEATURE_CHUNKS):
        rows_use(c)

    for half in range(2):
        shrink_out[half] = jnp.concatenate(
            [shrink[j][:, half * rank:(half + 1) * rank] for j in range(adapters)], axis=1
        ).reshape(n, CAP, adapters * rank)

    def back_copy(offset, other):
        to_core = sibling if other else core
        target = partner(me, offset)
        return pltpu.make_async_remote_copy(
            src_ref=shrink_out.at[to_core, target], dst_ref=shrink_in.at[core, me],
            send_sem=back_send.at[other, offset], recv_sem=back_recv.at[other, offset],
            device_id={"dp": target, "tensor": to_core}, device_id_type=MESH,
        )

    def back_arrival(offset, other):
        from_core = sibling if other else core
        source = partner(me, offset)
        return pltpu.make_async_remote_copy(
            src_ref=shrink_out.at[0, 0], dst_ref=shrink_in.at[from_core, source],
            send_sem=back_send.at[other, offset], recv_sem=back_recv.at[other, offset],
            device_id={"dp": source, "tensor": from_core}, device_id_type=MESH,
        )

    back = [(offset, other) for offset in order + [0] for other in range(2) if offset or other]
    for offset, other in back:
        back_copy(offset, other).start()
    shrink_in[core, me] = shrink_out[core, me]

    base_copy.wait()
    summed = total[core] + base_arrived[...]
    up_wait(len(steps) - 1)
    for offset, other in back:
        back_arrival(offset, other).wait_recv()

    got = jnp.concatenate([shrink_in[0, d] + shrink_in[1, d] for d in range(n)], axis=1)
    high = got.astype(jnp.bfloat16)
    low = (got - high.astype(jnp.float32)).astype(jnp.bfloat16)
    pick = jnp.where(
        position == lax.broadcasted_iota(jnp.int32, (rows, CAP), 1), 1.0, 0.0
    ).astype(jnp.bfloat16)
    mine = lax.broadcasted_iota(jnp.int32, (rows, n * adapters * rank), 1) // rank == chosen

    def spread(values):
        taken = jnp.dot(pick, values, preferred_element_type=jnp.float32)
        return jnp.where(mine, taken, 0.0).astype(jnp.bfloat16)

    spread_rows = jnp.concatenate([spread(high), spread(low)], axis=0)
    delta = jnp.dot(
        spread_rows, up[...].reshape(n * adapters * rank, lanes), preferred_element_type=jnp.float32
    )
    out_ref[...] = (summed + (delta[:rows] + delta[rows:])).astype(out_ref.dtype)

    for number in range(len(steps)):
        step, offsets = steps[number]
        for offset in offsets:
            up_copy(offset, step).wait_send()
    for c in range(FEATURE_CHUNKS):
        for offset in order:
            row_copy(c, offset).wait_send()
    for offset, other in back:
        back_copy(offset, other).wait_send()


def per_device(hidden, row_adapter_index, key_value_weight, adapter_down_weight, adapter_up_weight):
    n = lax.axis_size("dp")
    rows, width = hidden.shape
    adapters, _, ranks = adapter_down_weight.shape
    _, _, rank, lanes = adapter_up_weight.shape
    slots = adapters * CAP
    chunk = width // FEATURE_CHUNKS
    hbm = pl.BlockSpec(memory_space=pl.ANY)
    vmem = pl.BlockSpec(memory_space=pltpu.VMEM)
    dma = pltpu.SemaphoreType.DMA
    return pl.pallas_call(
        functools.partial(kernel, n),
        out_shape=jax.ShapeDtypeStruct((rows, lanes), jnp.bfloat16),
        in_specs=[vmem, hbm, hbm, hbm, hbm],
        out_specs=vmem,
        scratch_shapes=[
            pltpu.VMEM((rows, width), jnp.bfloat16),
            pltpu.VMEM(key_value_weight.shape, jnp.bfloat16),
            pltpu.VMEM(adapter_down_weight.shape, jnp.bfloat16),
            pltpu.VMEM((n, adapters * rank, lanes), jnp.bfloat16),
            pltpu.VMEM((FEATURE_CHUNKS, n, slots, chunk), jnp.bfloat16),
            pltpu.VMEM((FEATURE_CHUNKS, n, slots, chunk), jnp.bfloat16),
            pltpu.VMEM((2, rows, lanes), jnp.float32),
            pltpu.VMEM((rows, lanes), jnp.float32),
            pltpu.VMEM((adapters, n * CAP, ranks), jnp.float32),
            pltpu.VMEM((2, n, CAP, adapters * rank), jnp.float32),
            pltpu.VMEM((2, n, CAP, adapters * rank), jnp.float32),
            dma((FEATURE_CHUNKS,)),
            dma((WEIGHT_CHUNKS,)),
            dma,
            dma((adapters,)),
            dma((FEATURE_CHUNKS, n)),
            dma((FEATURE_CHUNKS, n)),
            dma((n,)),
            dma((n,)),
            dma((2, n)),
            dma((2, n)),
            dma,
            dma,
        ],
        compiler_params=pltpu.CompilerParams(
            collective_id=0, has_side_effects=True, vmem_limit_bytes=56 * 1024 * 1024
        ),
        cost_estimate=pl.CostEstimate(
            flops=2 * rows * width * 2 * lanes, bytes_accessed=20 * 1024 * 1024, transcendentals=0
        ),
    )(row_adapter_index, hidden, key_value_weight, adapter_down_weight, adapter_up_weight)


def solution(mesh):
    in_specs = (
        P(("groups", "dp"), "tensor"),
        P(("groups", "dp"), None),
        P("tensor", None),
        P(("groups", "dp"), "tensor", None),
        P(("groups", "dp"), None, None, None),
    )
    out_specs = P(("groups", "dp"), "tensor")
    return jax.shard_map(
        per_device, mesh=mesh, in_specs=in_specs, out_specs=out_specs, check_vma=False
    )
```

time: 130 us -> 91.2 us (0.70)
  the two profiles are of different devices: /device:TPU:0 before, /device:TPU:11 now
where the time goes in v1:
time: 91.2 us; the launch traced here: 91 us
  Pallas kernels  87.9 us (96%)
  local copies, waits for them, and re-layouts  3.06 us (3%)
    pallas_call x1, Pallas kernels, per_device(): pl.pallas_call(functools.partial(kernel, n), out_shape=jax.ShapeDtypeStru...  87.9 us
    unnamed x2, local copies, waits for them, and re-layouts  3.06 us

profile of v1, /device:TPU:11, one launch (start us, length us, event | category | flops | bytes accessed | tf_op | source)
XLA Modules:
  0.0 91.0 jit_solution(17349757611150287178)
XLA Ops:
  0.0 1.4 %copy.6.index_ref = s32[128,1]{1,0:T(8,128)} copy(s32[128,1]{0,1:T(1,128)} %param.6) | data formatting | bytes 1024 | tf_op args[1]
  1.4 87.9 %shard_map.55 = bf16[128,1024]{1,0:T(8,128)(2,1)} custom-call(s32[128,1]{1,0:T(8,128)} %copy.6.index_ref, bf16[128,4096]{1,0:T(8,128)(2,1)} %hidden_hbm.1, bf16[4096,2048]{1,0:T(8,128)(2,1)} %weight_hbm.1, bf16[2,4096,128]{2,1,0:T(8,128)(2,1)} %down_hbm.1, bf16[2,2,64,1024]{3,2,1,0:T(8,128)(2,1)} %up_hbm.1), custom_call_target="tpu_custom_call" | custom-call | flops 2147483648 | bytes 20971520 | tf_op jit(solution)/shard_map/pallas_call | solution.py:266
  89.3 1.7 %copy.8 = bf16[128,1024]{1,0:T(8,128)(2,1)} copy(bf16[128,1024]{1,0:T(8,128)(2,1)} %shard_map.55) | data formatting | bytes 524288

commit v2 on v1

--- a/solution.py
+++ b/solution.py
@@ -70,14 +70,15 @@
                     device_id={"dp": partner(me, offset), "tensor": sibling if other else core},
                 )
 
-    chosen = index_ref[...]
+    row_at = lax.broadcasted_iota(jnp.int32, (rows, rows), 0)
+    column_at = lax.broadcasted_iota(jnp.int32, (rows, rows), 1)
+    chosen = jnp.sum(
+        jnp.where(row_at == column_at, index_ref[...], 0), axis=1, keepdims=True
+    )
     one_hot = chosen == lax.broadcasted_iota(jnp.int32, (rows, adapters * n), 1)
     one_hot = jnp.where(one_hot, 1.0, 0.0)
-    below = lax.broadcasted_iota(jnp.int32, (rows, rows), 0) > lax.broadcasted_iota(
-        jnp.int32, (rows, rows), 1
-    )
     earlier = jnp.dot(
-        jnp.where(below, 1.0, 0.0).astype(jnp.bfloat16), one_hot.astype(jnp.bfloat16),
+        jnp.where(row_at > column_at, 1.0, 0.0).astype(jnp.bfloat16), one_hot.astype(jnp.bfloat16),
         preferred_element_type=jnp.float32,
     )
     position = jnp.sum(earlier * one_hot, axis=1, keepdims=True).astype(jnp.int32)
@@ -106,20 +107,20 @@
             device_id={"dp": partner(me, 1)}, device_id_type=MESH,
         )
 
-    steps = []
-    step = n // 2
-    while step:
-        steps.append((step, [step + held for held in range(0, n, 2 * step)]))
-        step //= 2
-
-    def up_start(number):
-        step, offsets = steps[number]
-        for offset in offsets:
-            up_copy(offset, step).start()
-
-    def up_wait(number):
-        for offset in steps[number][1]:
-            up_arrival(offset).wait_recv()
+    levels = [[] for _ in range(n.bit_length() - 1)]
+    for offset in reversed(range(0, n, 2)):
+        levels[offset.bit_count()].append(offset)
+
+    def up_forward(held):
+        last = held & -held if held else n
+        return [(held + step, step) for step in (2 ** e for e in reversed(range(n))) if step < last]
+
+    def up_level(number):
+        for held in levels[number]:
+            if held:
+                up_arrival(held).wait_recv()
+            for offset, step in up_forward(held):
+                up_copy(offset, step).start()
 
     order = sorted(range(1, n), reverse=True)
 
@@ -161,32 +162,32 @@
             else:
                 shrink[j] += part
 
-    up_start(0)
-    for c in range(FEATURE_CHUNKS):
-        rows_start(c)
-
-    for k in range(WEIGHT_CHUNKS):
-        weight_load(k).wait()
-        for half in range(2):
-            part = jnp.dot(
-                hidden[:, k * depth:(k + 1) * depth],
-                weight[k * depth:(k + 1) * depth, half * lanes:(half + 1) * lanes],
-                preferred_element_type=jnp.float32,
-            )
-            if k == 0:
-                total[half] = part
-            else:
-                total[half] += part
+    def base():
+        for k in range(WEIGHT_CHUNKS):
+            weight_load(k).wait()
+            for half in range(2):
+                part = jnp.dot(
+                    hidden[:, k * depth:(k + 1) * depth],
+                    weight[k * depth:(k + 1) * depth, half * lanes:(half + 1) * lanes],
+                    preferred_element_type=jnp.float32,
+                )
+                if k == 0:
+                    total[half] = part
+                else:
+                    total[half] += part
+        base_copy.start()
+
     base_copy = pltpu.make_async_remote_copy(
         src_ref=total.at[sibling], dst_ref=base_arrived, send_sem=base_send, recv_sem=base_recv,
         device_id={"tensor": sibling}, device_id_type=MESH,
     )
-    base_copy.start()
-
+    up_level(0)
+    for c in range(FEATURE_CHUNKS):
+        rows_start(c)
+    base()
     down_load.wait()
-    for number in range(len(steps) - 1):
-        up_wait(number)
-        up_start(number + 1)
+    for number in range(1, len(levels)):
+        up_level(number)
     for c in range(FEATURE_CHUNKS):
         rows_use(c)
 
@@ -220,7 +221,8 @@
 
     base_copy.wait()
     summed = total[core] + base_arrived[...]
-    up_wait(len(steps) - 1)
+    for offset in range(1, n, 2):
+        up_arrival(offset).wait_recv()
     for offset, other in back:
         back_arrival(offset, other).wait_recv()
 
@@ -242,9 +244,8 @@
     )
     out_ref[...] = (summed + (delta[:rows] + delta[rows:])).astype(out_ref.dtype)
 
-    for number in range(len(steps)):
-        step, offsets = steps[number]
-        for offset in offsets:
+    for held in range(n):
+        for offset, step in up_forward(held):
             up_copy(offset, step).wait_send()
     for c in range(FEATURE_CHUNKS):
         for offset in order:
@@ -299,7 +300,7 @@
         cost_estimate=pl.CostEstimate(
             flops=2 * rows * width * 2 * lanes, bytes_accessed=20 * 1024 * 1024, transcendentals=0
         ),
-    )(row_adapter_index, hidden, key_value_weight, adapter_down_weight, adapter_up_weight)
+    )(row_adapter_index.reshape(1, rows), hidden, key_value_weight, adapter_down_weight, adapter_up_weight)
 
 
 def solution(mesh):

time: 91.2 us -> 76.2 us (0.84)
  the two profiles are of different devices: /device:TPU:11 before, /device:TPU:0 now
where the time goes in v2:
time: 76.2 us; the launch traced here: 76.1 us
  Pallas kernels  74.4 us (98%)
  local copies, waits for them, and re-layouts  1.67 us (2%)
    pallas_call x1, Pallas kernels, per_device(): pl.pallas_call(functools.partial(kernel, n), out_shape=jax.ShapeDtypeStru...  74.4 us
    unnamed x1, local copies, waits for them, and re-layouts  1.67 us

profile of v2, /device:TPU:0, one launch (start us, length us, event | category | flops | bytes accessed | tf_op | source)
XLA Modules:
  0.0 76.1 jit_solution(17773653178268562828)
XLA Ops:
  0.0 74.4 %shard_map.55 = bf16[128,1024]{1,0:T(8,128)(2,1)} custom-call(s32[1,128]{1,0:T(1,128)} %bitcast.1, bf16[128,4096]{1,0:T(8,128)(2,1)} %hidden_hbm.1, bf16[4096,2048]{1,0:T(8,128)(2,1)} %weight_hbm.1, bf16[2,4096,128]{2,1,0:T(8,128)(2,1)} %down_hbm.1, bf16[2,2,64,1024]{3,2,1,0:T(8,128)(2,1)} %up_hbm.1), custom_call_target="tpu_custom_call" | custom-call | flops 2147483648 | bytes 20971520 | tf_op jit(solution)/shard_map/pallas_call | solution.py:267
  74.4 1.7 %copy.7 = bf16[128,1024]{1,0:T(8,128)(2,1)} copy(bf16[128,1024]{1,0:T(8,128)(2,1)} %shard_map.55) | data formatting | bytes 524288
